TPU v7x, 32 devices: a whole 2x2x4 slice. The times are simulated.
32 devices in a mesh: rep: 16 (over z, x, core), shard: 2 (over y).
Axes of the slice: x: 2, y: 2, z: 4, core: 2. Of those that a mesh axis runs over, the one named last changes fastest.
Arguments:
- inputs: bfloat16 [32, 512, 768], P('rep', 'shard'), may hold values from -6 to 6
- doc_lengths: int32 [32, 4], P('rep'), may hold values from 1 to 509, as said below
- qkv_weight: bfloat16 [768, 2304], P('shard'), may hold values from -0.3125 to 0.3125
- qv_bias: bfloat16 [1536], P('shard'), may hold values from -1.796875 to 1.796875
- out_weight: bfloat16 [768, 768], P('shard'), may hold values from -1.25 to 1.25
- out_bias: bfloat16 [768], P('shard'), may hold values from -1.796875 to 1.796875
- first_gain: bfloat16 [768], P('shard'), may hold values from 0.5 to 1.5
- first_shift: bfloat16 [768], P('shard'), may hold values from -1.796875 to 1.796875
- up_weight: bfloat16 [768, 3072], P('shard'), may hold values from -0.21875 to 0.21875
- up_bias: bfloat16 [3072], P('shard'), may hold values from -1.796875 to 1.796875
- down_weight: bfloat16 [3072, 768], P('shard'), may hold values from -0.15625 to 0.15625
- down_bias: bfloat16 [768], P('shard'), may hold values from -1.796875 to 1.796875
- second_gain: bfloat16 [768], P('shard'), may hold values from 0.5 to 1.5
- second_shift: bfloat16 [768], P('shard'), may hold values from -1.796875 to 1.796875
- grad_out: bfloat16 [32, 512, 768], P('rep', 'shard'), may hold values from -6 to 6
Outputs:
- layer_out: bfloat16 [32, 512, 768], P('rep', 'shard')
- input_grad: float32 [32, 512, 768], P('rep', 'shard')
- qkv_weight_grad: float32 [768, 2304], P('shard')
- qv_bias_grad: float32 [1536], P('shard')
- out_weight_grad: float32 [768, 768], P('shard')
- out_bias_grad: float32 [768], P('shard')
- first_gain_grad: float32 [768], P('shard')
- first_shift_grad: float32 [768], P('shard')
- up_weight_grad: float32 [768, 3072], P('shard')
- up_bias_grad: float32 [3072], P('shard')
- down_weight_grad: float32 [3072, 768], P('shard')
- down_bias_grad: float32 [768], P('shard')
- second_gain_grad: float32 [768], P('shard')
- second_shift_grad: float32 [768], P('shard')
Inputs may be any that keep to these rules, and one draw needn't show every extreme that they name: `doc_lengths`: each row lists in order the lengths of the 4 documents packed into one sequence; a row sums to 512.
All inputs are finite; a program needn't handle non-finite values.
Results may differ from a plain program's by a relative error of at most 0.014.
The roundings to bfloat16 on the way count: a program that leaves them out, or rounds other values in their place, can miss the bound.
Values may be sent and summed in bfloat16 or wider, within the bound.
A program may use at most 192 MiB of HBM per device.

v0:
```python
import math

import jax
import jax.numpy as jnp
from jax import lax
from jax.sharding import PartitionSpec as P

HEADS = 12


norm_eps = 1e-05


def norm_forward(values, gain, shift):
    center = values - jnp.mean(values, axis=-1, keepdims=True)
    spread = jnp.mean(center * center, axis=-1, keepdims=True)
    scaler = lax.rsqrt(spread + norm_eps)
    normed = center * scaler
    return (normed * gain + shift, normed, scaler)


def norm_backward(grad, normed, scaler, gain):
    scaled = grad * gain
    inner = scaled - jnp.mean(scaled, axis=-1, keepdims=True)
    inner = inner - normed * jnp.mean(scaled * normed, axis=-1, keepdims=True)
    return inner * scaler


def column_sums(values):
    return jnp.sum(values.astype(jnp.float32), axis=0)


def back_scores(query_seq, keys_seq, values_seq, doc_rows, doc_cols, logsum_seq, grad_seq, scale):
    scores = (
        jnp.einsum("qhd,khd->hqk", query_seq, keys_seq, preferred_element_type=jnp.float32) * scale
    )
    same = (doc_rows[:, None] == doc_cols[None, :])[None]
    probs = jnp.where(same, jnp.exp(scores - logsum_seq), 0.0)
    grad_probs = jnp.einsum(
        "qhd,khd->hqk", grad_seq, values_seq, preferred_element_type=jnp.float32
    )
    return (probs, grad_probs)


def local(
    inputs,
    doc_lengths,
    qkv_weight,
    qv_bias,
    out_weight,
    out_bias,
    first_gain,
    first_shift,
    up_weight,
    up_bias,
    down_weight,
    down_bias,
    second_gain,
    second_shift,
    grad_out,
):
    seqs, rows, width = inputs.shape
    parts = lax.axis_size("shard")
    full_len = rows * parts
    head_dim = width // HEADS
    scale = 1.0 / math.sqrt(head_dim)
    ends = jnp.cumsum(doc_lengths, axis=1)
    spots = jnp.arange(full_len, dtype=jnp.int32)
    doc_all = jnp.sum((ends[:, :, None] <= spots[None, None, :]).astype(jnp.int32), axis=1)
    doc_own = lax.dynamic_slice_in_dim(doc_all, lax.axis_index("shard") * rows, rows, 1)
    gathered = (
        lax.all_gather(qkv_weight, "shard", axis=0, tiled=True),
        lax.all_gather(qv_bias, "shard", axis=0, tiled=True),
        lax.all_gather(out_weight, "shard", axis=0, tiled=True),
        lax.all_gather(out_bias, "shard", axis=0, tiled=True),
        lax.all_gather(first_gain, "shard", axis=0, tiled=True),
        lax.all_gather(first_shift, "shard", axis=0, tiled=True),
        lax.all_gather(up_weight, "shard", axis=0, tiled=True),
        lax.all_gather(up_bias, "shard", axis=0, tiled=True),
        lax.all_gather(down_weight, "shard", axis=0, tiled=True),
        lax.all_gather(down_bias, "shard", axis=0, tiled=True),
        lax.all_gather(second_gain, "shard", axis=0, tiled=True),
        lax.all_gather(second_shift, "shard", axis=0, tiled=True),
    )
    (
        full_qkv,
        full_qv,
        full_out,
        full_outb,
        full_g1,
        full_s1,
        full_up,
        full_upb,
        full_down,
        full_downb,
        full_g2,
        full_s2,
    ) = gathered
    flat = inputs.reshape(seqs * rows, width)
    bias = jnp.concatenate(
        [
            full_qv[:width].astype(jnp.float32),
            jnp.zeros((width,), jnp.float32),
            full_qv[width:].astype(jnp.float32),
        ]
    )
    qkv = (jnp.dot(flat, full_qkv, preferred_element_type=jnp.float32) + bias).astype(jnp.bfloat16)
    query_flat = qkv[:, :width].reshape(seqs, rows, width)
    query = query_flat.reshape(seqs, rows, HEADS, head_dim)
    keys_own = qkv[:, width : 2 * width].reshape(seqs, rows, width)
    values_own = qkv[:, 2 * width :].reshape(seqs, rows, width)
    keys_all, values_all = (
        lax.all_gather(keys_own, "shard", axis=1, tiled=True),
        lax.all_gather(values_own, "shard", axis=1, tiled=True),
    )
    keys_all = keys_all.reshape(seqs, full_len, HEADS, head_dim)
    values_all = values_all.reshape(seqs, full_len, HEADS, head_dim)

    def attend(item):
        query_seq, keys_seq, values_seq, doc_rows, doc_cols = item
        scores = (
            jnp.einsum("qhd,khd->hqk", query_seq, keys_seq, preferred_element_type=jnp.float32)
            * scale
        )
        same = (doc_rows[:, None] == doc_cols[None, :])[None]
        masked = jnp.where(same, scores, -1000000000.0)
        top = jnp.max(masked, axis=-1, keepdims=True)
        expo = jnp.exp(masked - top)
        total = jnp.sum(expo, axis=-1, keepdims=True)
        probs_low = (expo / total).astype(jnp.bfloat16)
        mixed_seq = jnp.einsum(
            "hqk,khd->qhd", probs_low, values_seq, preferred_element_type=jnp.float32
        )
        return (mixed_seq.astype(jnp.bfloat16), top + jnp.log(total))

    mixed, logsum = lax.map(attend, (query, keys_all, values_all, doc_own, doc_all))
    mixed_flat = mixed.reshape(seqs * rows, width)
    attended = jnp.dot(mixed_flat, full_out, preferred_element_type=jnp.float32) + full_outb.astype(
        jnp.float32
    )
    first_norm, first_normed, first_scaler = norm_forward(
        flat.astype(jnp.float32) + attended,
        full_g1.astype(jnp.float32),
        full_s1.astype(jnp.float32),
    )
    first_low = first_norm.astype(jnp.bfloat16)
    hidden = jnp.dot(first_low, full_up, preferred_element_type=jnp.float32) + full_upb.astype(
        jnp.float32
    )
    active = jax.nn.gelu(hidden, approximate=False).astype(jnp.bfloat16)
    branch = jnp.dot(active, full_down, preferred_element_type=jnp.float32) + full_downb.astype(
        jnp.float32
    )
    second_out, second_normed, second_scaler = norm_forward(
        first_norm + branch, full_g2.astype(jnp.float32), full_s2.astype(jnp.float32)
    )
    layer_out = second_out.astype(jnp.bfloat16).reshape(seqs, rows, width)
    back_qkv, back_out, back_g1, back_up, back_down, back_g2 = (
        full_qkv,
        full_out,
        full_g1,
        full_up,
        full_down,
        full_g2,
    )
    cotangent = grad_out.reshape(seqs * rows, width).astype(jnp.float32)
    second_gain_grad = jnp.sum(cotangent * second_normed, axis=0)
    second_shift_grad = jnp.sum(cotangent, axis=0)
    grad_second = norm_backward(
        cotangent, second_normed, second_scaler, back_g2.astype(jnp.float32)
    )
    grad_branch = grad_second.astype(jnp.bfloat16)
    down_weight_grad = jnp.einsum(
        "tf,td->fd", active, grad_branch, preferred_element_type=jnp.float32
    )
    down_bias_grad = column_sums(grad_branch)
    grad_active = jnp.einsum(
        "td,fd->tf", grad_branch, back_down, preferred_element_type=jnp.float32
    )
    normal_cdf = 0.5 * (1.0 + lax.erf(hidden * 0.7071067811865476))
    normal_pdf = jnp.exp(-0.5 * hidden * hidden) * 0.3989422804014327
    grad_hidden = (grad_active * (normal_cdf + hidden * normal_pdf)).astype(jnp.bfloat16)
    up_weight_grad = jnp.einsum(
        "td,tf->df", first_low, grad_hidden, preferred_element_type=jnp.float32
    )
    up_bias_grad = column_sums(grad_hidden)
    grad_first_norm = grad_second + jnp.einsum(
        "tf,df->td", grad_hidden, back_up, preferred_element_type=jnp.float32
    )
    first_gain_grad = jnp.sum(grad_first_norm * first_normed, axis=0)
    first_shift_grad = jnp.sum(grad_first_norm, axis=0)
    grad_first = norm_backward(
        grad_first_norm, first_normed, first_scaler, back_g1.astype(jnp.float32)
    )
    grad_attended = grad_first.astype(jnp.bfloat16)
    out_weight_grad = jnp.einsum(
        "td,te->de", mixed_flat, grad_attended, preferred_element_type=jnp.float32
    )
    out_bias_grad = column_sums(grad_attended)
    grad_mixed = jnp.einsum(
        "te,de->td", grad_attended, back_out, preferred_element_type=jnp.float32
    )
    grad_mixed_flat = grad_mixed.astype(jnp.bfloat16).reshape(seqs, rows, width)
    grad_mixed = grad_mixed_flat.reshape(seqs, rows, HEADS, head_dim)

    def attend_back(item):
        query_seq, keys_seq, values_seq, doc_rows, doc_cols, logsum_seq, grad_seq = item
        probs, grad_probs = back_scores(
            query_seq, keys_seq, values_seq, doc_rows, doc_cols, logsum_seq, grad_seq, scale
        )
        probs_low = probs.astype(jnp.bfloat16)
        inner = jnp.sum(probs * grad_probs, axis=-1, keepdims=True)
        grad_scores = (probs * (grad_probs - inner)).astype(jnp.bfloat16)
        grad_query = (
            jnp.einsum("hqk,khd->qhd", grad_scores, keys_seq, preferred_element_type=jnp.float32)
            * scale
        )
        grad_keys = (
            jnp.einsum("hqk,qhd->khd", grad_scores, query_seq, preferred_element_type=jnp.float32)
            * scale
        )
        grad_values = jnp.einsum(
            "hqk,qhd->khd", probs_low, grad_seq, preferred_element_type=jnp.float32
        )
        return (grad_query, grad_keys, grad_values)

    grad_query, grad_keys, grad_values = lax.map(
        attend_back, (query, keys_all, values_all, doc_own, doc_all, logsum, grad_mixed)
    )
    grad_keys = grad_keys.reshape(seqs, full_len, width)
    grad_values = grad_values.reshape(seqs, full_len, width)
    grad_keys, grad_values = (
        lax.psum_scatter(grad_keys, "shard", scatter_dimension=1, tiled=True),
        lax.psum_scatter(grad_values, "shard", scatter_dimension=1, tiled=True),
    )
    grad_qkv = jnp.concatenate(
        [
            grad_query.reshape(seqs * rows, width),
            grad_keys.reshape(seqs * rows, width),
            grad_values.reshape(seqs * rows, width),
        ],
        axis=1,
    ).astype(jnp.bfloat16)
    qkv_weight_grad = jnp.einsum("td,te->de", flat, grad_qkv, preferred_element_type=jnp.float32)
    qkv_sums = column_sums(grad_qkv)
    qv_bias_grad = jnp.concatenate([qkv_sums[:width], qkv_sums[2 * width :]])
    input_grad = grad_first + jnp.einsum(
        "te,de->td", grad_qkv, back_qkv, preferred_element_type=jnp.float32
    )
    input_grad = input_grad.reshape(seqs, rows, width)
    owned = (
        lax.psum_scatter(qkv_weight_grad, "shard", scatter_dimension=0, tiled=True),
        lax.psum_scatter(qv_bias_grad, "shard", scatter_dimension=0, tiled=True),
        lax.psum_scatter(out_weight_grad, "shard", scatter_dimension=0, tiled=True),
        lax.psum_scatter(out_bias_grad, "shard", scatter_dimension=0, tiled=True),
        lax.psum_scatter(first_gain_grad, "shard", scatter_dimension=0, tiled=True),
        lax.psum_scatter(first_shift_grad, "shard", scatter_dimension=0, tiled=True),
        lax.psum_scatter(up_weight_grad, "shard", scatter_dimension=0, tiled=True),
        lax.psum_scatter(up_bias_grad, "shard", scatter_dimension=0, tiled=True),
        lax.psum_scatter(down_weight_grad, "shard", scatter_dimension=0, tiled=True),
        lax.psum_scatter(down_bias_grad, "shard", scatter_dimension=0, tiled=True),
        lax.psum_scatter(second_gain_grad, "shard", scatter_dimension=0, tiled=True),
        lax.psum_scatter(second_shift_grad, "shard", scatter_dimension=0, tiled=True),
    )
    (
        own_qkv,
        own_qv,
        own_out,
        own_outb,
        own_g1,
        own_s1,
        own_up,
        own_upb,
        own_down,
        own_downb,
        own_g2,
        own_s2,
    ) = owned
    banded = (
        lax.psum_scatter(own_qkv, "rep", scatter_dimension=1, tiled=True),
        lax.psum_scatter(own_out, "rep", scatter_dimension=1, tiled=True),
        lax.psum_scatter(own_up, "rep", scatter_dimension=1, tiled=True),
        lax.psum_scatter(own_down, "rep", scatter_dimension=1, tiled=True),
    )
    matrices = (
        lax.all_gather(banded[0], "rep", axis=1, tiled=True),
        lax.all_gather(banded[1], "rep", axis=1, tiled=True),
        lax.all_gather(banded[2], "rep", axis=1, tiled=True),
        lax.all_gather(banded[3], "rep", axis=1, tiled=True),
    )
    smalls = lax.psum((own_qv, own_outb, own_g1, own_s1, own_upb, own_downb, own_g2, own_s2), "rep")
    return (
        layer_out,
        input_grad,
        matrices[0],
        smalls[0],
        matrices[1],
        smalls[1],
        smalls[2],
        smalls[3],
        matrices[2],
        smalls[4],
        matrices[3],
        smalls[5],
        smalls[6],
        smalls[7],
    )


def solution(mesh):
    return jax.shard_map(
        local,
        mesh=mesh,
        in_specs=(
            P("rep", "shard", None),
            P("rep", None),
            P("shard", None),
            P("shard"),
            P("shard", None),
            P("shard"),
            P("shard"),
            P("shard"),
            P("shard", None),
            P("shard"),
            P("shard", None),
            P("shard"),
            P("shard"),
            P("shard"),
            P("rep", "shard", None),
        ),
        out_specs=(
            P("rep", "shard", None),
            P("rep", "shard", None),
            P("shard", None),
            P("shard"),
            P("shard", None),
            P("shard"),
            P("shard"),
            P("shard"),
            P("shard", None),
            P("shard"),
            P("shard", None),
            P("shard"),
            P("shard"),
            P("shard"),
        ),
        check_vma=False,
    )
```

profile of v0, /device:TPU:0, one launch (start us, length us, event | category | flops | bytes accessed | tf_op | source)
XLA Modules:
  0.0 1266.3 jit_solution(5007584185611888521)
XLA Ops:
  8.6 5.2 all-gather
  13.9 47.7 %all-gather.19.cloned.1.call-done = bf16[768,2304]{1,0:T(8,128)(2,1)} async-done(((bf16[384,2304]{1,0:T(8,128)(2,1)}), bf16[768,2304]{1,0:T(8,128)(2,1)}) %all-gather.19.cloned.1.call-update) | async-done | bytes 3538960 | tf_op jit(solution)/shard_map/all_gather | solution.py:72
  61.7 4.2 fusion.67
  70.2 4.3 all-gather.1
  74.6 4.3 all-gather.2
  79.0 4.3 all-gather.3
  83.4 4.5 all-gather.4
  87.9 4.3 all-gather.5
  92.3 4.3 all-gather.6
  97.6 4.3 all-gather.7
  102.6 2.7 copy.83
  105.2 19.0 %all-gather.23.cloned.1.call-done = bf16[2,512,768]{2,1,0:T(8,128)(2,1)} async-done(((bf16[2,256,768]{2,1,0:T(8,128)(2,1)}), bf16[2,512,768]{2,1,0:T(8,128)(2,1)}) %all-gather.23.cloned.1.call-update) | async-done | bytes 1572880 | tf_op jit(solution)/shard_map/all_gather | solution.py:113
  126.0 13.4 %while.26 = (s32[]{:T(128)}, bf16[2,256,12,64]{1,3,2,0:T(8,128)(2,1)}, f32[2,12,256,1]{2,1,3,0:T(8,128)S(1)}, bf16[2,512,12,64]{1,3,2,0:T(8,128)(2,1)}, s32[2,25...) while((s32[]{:T(128)}, ...), condition=%wide.region_5.6_spmd, body=%wide.region_2.5_spmd.sunk | while | flops 421852160 | bytes 28179588 | solution.py:136
  129.3 3.4 fusion.128
  135.9 3.4 fusion.128
  142.3 6.1 all-gather.25.cloned.1.call-done
  152.6 60.0 %all-gather.27.cloned.1.call-done = bf16[768,3072]{1,0:T(8,128)(2,1)} async-done(((bf16[384,3072]{1,0:T(8,128)(2,1)}), bf16[768,3072]{1,0:T(8,128)(2,1)}) %all-gather.27.cloned.1.call-update) | async-done | bytes 4718608 | tf_op jit(solution)/shard_map/all_gather | solution.py:78
  212.6 20.6 %fusion.53 = (bf16[512,3072]{1,0:T(8,128)(2,1)}, f32[512,3072]{1,0:T(8,128)}) fusion(f32[3072]{0:T(1024)S(1)} %bitcast.204, bf16[768,3072]{1,0:T(8,128)(2,1)} %all-gather.27.cloned.1.call-done, f32[512,768]{1,0:T(8,128)} %copy-done.5, f32[768]{0:T(1024)S(1)} %reshape.252, f32[768]{0:T(1024)S(1)} %reshape.251, f32[512]{0:T(512)S(1)} %add_rsqrt_fusion.1, ...), kind=kOutput, calls=%fused_computation.69 | convolution fusion | flops 2521694208 | bytes 15751168 | tf_op jit(solution)/shard_map/dot_general | solution.py:147
  233.2 43.5 %all-gather.29.cloned.1.call-done = bf16[3072,768]{1,0:T(8,128)(2,1)} async-done(((bf16[1536,768]{1,0:T(8,128)(2,1)}), bf16[3072,768]{1,0:T(8,128)(2,1)}) %all-gather.29.cloned.1.call-update) | async-done | bytes 4718608 | tf_op jit(solution)/shard_map/all_gather | solution.py:80
  276.7 6.6 fusion.92
  286.1 4.9 convert_reduce_fusion
  291.0 3.1 multiply_reduce_fusion.1
  301.4 23.7 %while.27 = (s32[]{:T(128)}, bf16[2,256,12,64]{1,3,2,0:T(8,128)(2,1)}, f32[2,512,12,64]{1,3,2,0:T(8,128)}, f32[2,512,12,64]{1,3,2,0:T(8,128)}, bf16[2,512,12,64]...) while((s32[]{:T(128)}, ...), condition=%wide.region_16.17_spmd, body=%wide.region_14.16_spmd.sunk | while | flops 1030943744 | bytes 93432080 | solution.py:227
  330.2 38.4 %reduce-scatter.17.cloned.1.call-done = f32[2,256,768]{1,2,0:T(8,128)} async-done(((f32[2,512,768]{1,2,0:T(8,128)}), f32[2,256,768]{1,2,0:T(8,128)}) %reduce-scatter.17.cloned.1.call-update) | async-done | bytes 1572880 | tf_op jit(solution)/shard_map/reduce_scatter | solution.py:233
  373.6 41.3 %reduce-scatter.19.cloned.1.call-done = f32[2,256,768]{1,2,0:T(8,128)} async-done(((f32[2,512,768]{1,2,0:T(8,128)}), f32[2,256,768]{1,2,0:T(8,128)}) %reduce-scatter.19.cloned.1.call-update) | async-done | bytes 1572880 | tf_op jit(solution)/shard_map/reduce_scatter | solution.py:234
  419.9 6.5 convolution_bitcast_fusion
  427.8 7.2 fusion.84
  436.3 8.2 fusion.81
  444.6 7.3 reduce-scatter.25.cloned.1.call-done
  454.6 85.2 %reduce-scatter.21.cloned.1.call-done = f32[384,2304]{0,1:T(8,128)} async-done(((f32[768,2304]{0,1:T(8,128)}), f32[384,2304]{0,1:T(8,128)}) %reduce-scatter.21.cloned.1.call-update) | async-done | bytes 3538960 | tf_op jit(solution)/shard_map/reduce_scatter | solution.py:252
  539.9 112.8 %reduce-scatter.27.cloned.1.call-done = f32[384,3072]{1,0:T(8,128)} async-done(((f32[768,3072]{1,0:T(8,128)}), f32[384,3072]{1,0:T(8,128)}) %reduce-scatter.27.cloned.1.call-update) | async-done | bytes 4718608 | tf_op jit(solution)/shard_map/reduce_scatter | solution.py:258
  652.7 6.0 copy.105
  658.8 106.6 %reduce-scatter.29.cloned.1.call-done = f32[1536,768]{1,0:T(8,128)} async-done(((f32[3072,768]{1,0:T(8,128)}), f32[1536,768]{1,0:T(8,128)}) %reduce-scatter.29.cloned.1.call-update) | async-done | bytes 4718608 | tf_op jit(solution)/shard_map/reduce_scatter | solution.py:260
  765.4 6.0 copy.107
  771.5 56.2 %reduce-scatter.31.cloned.1.call-done = f32[48,384]{1,0:T(8,128)} async-done(((f32[768,384]{1,0:T(8,128)}), f32[48,384]{1,0:T(8,128)}) %reduce-scatter.31.cloned.1.call-update) | async-done | bytes 73744
  827.8 70.7 %reduce-scatter.23.cloned.1.call-done = f32[384,144]{0,1:T(8,128)} async-done(((f32[384,2304]{0,1:T(8,128)}), f32[384,144]{0,1:T(8,128)}) %reduce-scatter.23.cloned.1.call-update) | async-done | bytes 221200 | tf_op jit(solution)/shard_map/reduce_scatter | solution.py:280
  898.5 78.8 %reduce-scatter.33.cloned.1.call-done = f32[192,384]{1,0:T(8,128)} async-done(((f32[3072,384]{1,0:T(8,128)}), f32[192,384]{1,0:T(8,128)}) %reduce-scatter.33.cloned.1.call-update) | async-done | bytes 294928
  977.4 79.3 %reduce-scatter.35.cloned.1.call-done = f32[48,1536]{1,0:T(8,128)} async-done(((f32[768,1536]{1,0:T(8,128)}), f32[48,1536]{1,0:T(8,128)}) %reduce-scatter.35.cloned.1.call-update) | async-done | bytes 294928
  1060.8 8.6 all-reduce.9
  1070.1 58.5 %all-reduce.8 = (f32[768]{0:T(1024)}, f32[384]{0:T(512)}, f32[384]{0:T(512)}, f32[384]{0:T(512)}, f32[1536]{0:T(1024)}, /*index=5*/f32[384]{0:T(512)}, f32[384]{0:T(512)}, f32[384]{0:T(512)}) all-reduce(f32[768]{0:T(1024)S(1)} %dynamic-slice.1, f32[384]{0:T(512)S(1)} %dynamic-slice.3, ...), channel_id=1, replica_groups=mesh['rep'=16,'shard'=2] {'rep'}, use_global_device_ids=true, to_apply=%region_23.24 | all-reduce | flops 4608 | bytes 36864 | tf_op jit(solution)/shard_map/psum | solution.py:291
  1128.6 5.5 convolution_add_fusion.1
  1134.1 2.7 copy.100
  1136.7 7.8 all-gather.31.cloned.1.call-done
  1144.5 5.2 copy.99
  1149.6 49.4 %all-gather.35.cloned.1.call-done = f32[384,3072]{0,1:T(8,128)} async-done(((f32[384,192]{0,1:T(8,128)}), f32[384,3072]{0,1:T(8,128)}) %all-gather.35.cloned.1.call-update) | async-done | bytes 4718608 | tf_op jit(solution)/shard_map/all_gather | solution.py:288
  1199.0 6.0 copy.101
  1205.1 47.9 %all-gather.37.cloned.1.call-done = f32[1536,768]{0,1:T(8,128)} async-done(((f32[1536,48]{0,1:T(8,128)}), f32[1536,768]{0,1:T(8,128)}) %all-gather.37.cloned.1.call-update) | async-done | bytes 4718608 | tf_op jit(solution)/shard_map/all_gather | solution.py:289
  1253.0 6.0 copy.102
  (237 shorter events, 79.6 us)
Async XLA Ops:
  7.2 54.5 %all-gather.19.cloned.1.call-start = ((), (), s32[]{:S(2)}) async-start(), calls=%async_computation.10 | async-start | bytes 5308416 | tf_op jit(solution)/shard_map/all_gather | solution.py:72
  7.9 94.7 %all-gather.21.cloned.1.call-start = ((), (), s32[]{:S(2)}) async-start(), calls=%async_computation.11 | async-start | bytes 2359296 | tf_op jit(solution)/shard_map/all_gather | solution.py:114
  67.2 2.7 copy-start.21
  67.2 2.9 copy-start.22
  67.2 7.3 copy-start.23
  67.2 11.7 copy-start.24
  67.2 16.1 %copy-start.20 = (bf16[1536]{0:T(1024)(128)(2,1)S(1)}, bf16[1536]{0:T(1024)(128)(2,1)}, u32[]{:S(2)}) copy-start(bf16[1536]{0:T(1024)(128)(2,1)} %param.28) | copy-start | bytes 9220
  67.2 20.6 %copy-start.25 = (bf16[384]{0:T(512)(128)(2,1)S(1)}, bf16[384]{0:T(512)(128)(2,1)}, u32[]{:S(2)}) copy-start(bf16[384]{0:T(512)(128)(2,1)} %param.30) | copy-start | bytes 2308
  67.2 25.0 %copy-start.26 = (bf16[384]{0:T(512)(128)(2,1)S(1)}, bf16[384]{0:T(512)(128)(2,1)}, u32[]{:S(2)}) copy-start(bf16[384]{0:T(512)(128)(2,1)} %param.31) | copy-start | bytes 2308
  67.3 29.4 %copy-start.2 = (bf16[2,256,768]{2,1,0:T(8,128)(2,1)S(1)}, bf16[2,256,768]{2,1,0:T(8,128)(2,1)}, u32[]{:S(2)}) copy-start(bf16[2,256,768]{2,1,0:T(8,128)(2,1)} %param.33) | copy-start | bytes 2359300
  67.3 57.0 %all-gather.23.cloned.1.call-start = ((), (), s32[]{:S(2)}) async-start(), calls=%async_computation.12 | async-start | bytes 2359296 | tf_op jit(solution)/shard_map/all_gather | solution.py:113
  67.3 30.2 %copy-start.27 = (bf16[384]{0:T(512)(128)(2,1)S(1)}, bf16[384]{0:T(512)(128)(2,1)}, u32[]{:S(2)}) copy-start(bf16[384]{0:T(512)(128)(2,1)} %param.32) | copy-start | bytes 2308
  68.0 80.4 %all-gather.25.cloned.1.call-start = ((), (), s32[]{:S(2)}) async-start(), calls=%async_computation.13 | async-start | bytes 1769472 | tf_op jit(solution)/shard_map/all_gather | solution.py:74
  68.6 144.0 %all-gather.27.cloned.1.call-start = ((), (), s32[]{:S(2)}) async-start(), calls=%async_computation.14 | async-start | bytes 7077888 | tf_op jit(solution)/shard_map/all_gather | solution.py:78
  69.2 207.5 %all-gather.29.cloned.1.call-start = ((), (), s32[]{:S(2)}) async-start(), calls=%async_computation.15 | async-start | bytes 7077888 | tf_op jit(solution)/shard_map/all_gather | solution.py:80
  69.8 298.9 %reduce-scatter.17.cloned.1.call-start = ((), (), s32[]{:S(2)}) async-start(), calls=%async_computation.16 | async-start | bytes 4718592 | tf_op jit(solution)/shard_map/reduce_scatter | solution.py:233
  127.5 1.8 copy-start
  134.1 1.8 copy-start
  276.7 9.4 copy-start.32
  283.6 2.4 copy-start.28
  284.3 6.7 slice-start
  286.0 5.0 copy-start.3
  286.0 5.0 copy-start.6
  286.0 5.0 slice-start.1
  291.0 3.2 copy-start.31
  294.2 1.7 copy-start.29
  305.4 2.1 copy-start.11
  308.2 1.7 copy-start.12
  317.3 2.1 copy-start.11
  325.1 89.8 %reduce-scatter.19.cloned.1.call-start = ((), (), s32[]{:S(2)}) async-start(), calls=%async_computation.17 | async-start | bytes 4718592 | tf_op jit(solution)/shard_map/reduce_scatter | solution.py:234
  325.9 3.3 copy-start.18
  325.9 126.0 %reduce-scatter.25.cloned.1.call-start = ((), (), s32[]{:S(2)}) async-start(), calls=%async_computation.21 | async-start | bytes 3538944 | tf_op jit(solution)/shard_map/reduce_scatter | solution.py:254
  328.9 210.8 %reduce-scatter.21.cloned.1.call-start = ((), (), s32[]{:S(2)}) async-start(), calls=%async_computation.18 | async-start | bytes 10616832 | tf_op jit(solution)/shard_map/reduce_scatter | solution.py:252
  330.2 89.6 %copy-start.13 = (bf16[96,8,2,256]{3,1,2,0:T(8,128)(2,1)}, bf16[96,8,2,256]{3,1,2,0:T(8,128)(2,1)S(1)}, u32[]{:S(2)}) copy-start(bf16[96,8,2,256]{3,1,2,0:T(8,128)(2,1)S(1)} %copy.111) | copy-start | bytes 2359300
  426.4 226.3 %reduce-scatter.27.cloned.1.call-start = ((), (), s32[]{:S(2)}) async-start(), calls=%async_computation.23 | async-start | bytes 14155776 | tf_op jit(solution)/shard_map/reduce_scatter | solution.py:258
  435.0 330.4 %reduce-scatter.29.cloned.1.call-start = ((), (), s32[]{:S(2)}) async-start(), calls=%async_computation.25 | async-start | bytes 14155776 | tf_op jit(solution)/shard_map/reduce_scatter | solution.py:260
  444.6 383.1 %reduce-scatter.31.cloned.1.call-start = ((), (), s32[]{:S(2)}) async-start(), calls=%async_computation.27 | async-start | bytes 1253376
  454.6 443.9 %reduce-scatter.23.cloned.1.call-start = ((), (), s32[]{:S(2)}) async-start(), calls=%async_computation.19 | async-start | bytes 3760128 | tf_op jit(solution)/shard_map/reduce_scatter | solution.py:280
  539.8 437.5 %reduce-scatter.33.cloned.1.call-start = ((), (), s32[]{:S(2)}) async-start(), calls=%async_computation.28 | async-start | bytes 5013504
  658.7 398.0 %reduce-scatter.35.cloned.1.call-start = ((), (), s32[]{:S(2)}) async-start(), calls=%async_computation.29 | async-start | bytes 5013504
  771.5 285.3 %copy-start.30 = (u32[32]{0:T(128)S(1)}, u32[32]{0:T(128)}, u32[]{:S(2)}) copy-start(u32[32]{0:T(128)} %constant.151) | copy-start | bytes 388
  771.5 287.8 %copy-start.14 = (bf16[96,8,2,256]{3,1,2,0:T(8,128)(2,1)S(1)}, bf16[96,8,2,256]{3,1,2,0:T(8,128)(2,1)}, u32[]{:S(2)}) copy-start(bf16[96,8,2,256]{3,1,2,0:T(8,128)(2,1)} %copy-done.13) | copy-start | bytes 2359300
  771.5 287.8 %copy-start.15 = (bf16[512,768]{0,1:T(8,128)(2,1)S(1)}, bf16[512,768]{0,1:T(8,128)(2,1)}, u32[]{:S(2)}) copy-start(bf16[512,768]{0,1:T(8,128)(2,1)} %copy.94) | copy-start | bytes 2359300
  771.5 289.4 %copy-start.19 = (f32[768]{0:T(1024)S(1)}, f32[768]{0:T(1024)}, u32[]{:S(2)}) copy-start(f32[768]{0:T(1024)} %get-tuple-element.292) | copy-start | bytes 9220
  771.5 362.6 %all-gather.33.cloned.1.call-start = ((), (), s32[]{:S(2)}) async-start(), calls=%async_computation.22 | async-start | bytes 1253376 | tf_op jit(solution)/shard_map/all_gather | solution.py:287
  827.7 316.8 %all-gather.31.cloned.1.call-start = ((), (), s32[]{:S(2)}) async-start(), calls=%async_computation.20 | async-start | bytes 3760128 | tf_op jit(solution)/shard_map/all_gather | solution.py:286
  898.5 300.5 %all-gather.35.cloned.1.call-start = ((), (), s32[]{:S(2)}) async-start(), calls=%async_computation.24 | async-start | bytes 5013504 | tf_op jit(solution)/shard_map/all_gather | solution.py:288
  977.3 275.6 %all-gather.37.cloned.1.call-start = ((), (), s32[]{:S(2)}) async-start(), calls=%async_computation.26 | async-start | bytes 5013504 | tf_op jit(solution)/shard_map/all_gather | solution.py:289
  (13 other events, 16.7 us)
Sparse Core Ops, SparseCore 0:
  9.6 52.0 all-gather.18
  67.4 27.4 all-gather.20
  97.0 27.2 all-gather.22
  125.7 22.7 all-gather.24
  149.9 62.6 all-gather.26
  214.0 62.6 all-gather.28
  325.2 43.3 reduce-scatter.16
  371.5 43.3 reduce-scatter.18
  417.1 34.7 reduce-scatter.24
  454.1 85.5 reduce-scatter.20
  542.1 110.5 reduce-scatter.26
  654.8 110.5 reduce-scatter.28
  769.6 58.0 reduce-scatter.30
  831.4 66.9 reduce-scatter.22
  902.7 74.5 reduce-scatter.32
  982.1 74.5 reduce-scatter.34
  1058.8 37.4 all-gather.32
  1098.5 45.9 all-gather.30
  1146.8 52.2 all-gather.34
  1201.2 51.7 all-gather.36
where the time goes:
time: 1270 us
  waiting for transfers between devices  962 us (76%)
  blocking collectives  103 us (8%)
  matrix products  98.3 us (8%)
  local copies, waits for them, and re-layouts  65.3 us (5%)
  other arithmetic  19.3 us (2%)
  between operations  17.3 us (1%)
    unnamed x23, waiting for transfers between devices  218 us
    reduce_scatter x1, waiting for transfers between devices, local(): lax.psum_scatter(up_weight_grad, 'shard', scatter_dimension=0, tiled=True)  113 us
    reduce_scatter x1, waiting for transfers between devices, local(): lax.psum_scatter(down_weight_grad, 'shard', scatter_dimension=0, tiled=True)  107 us
    reduce_scatter x1, waiting for transfers between devices, local(): lax.psum_scatter(qkv_weight_grad, 'shard', scatter_dimension=0, tiled=True)  85.2 us
    reduce_scatter x1, waiting for transfers between devices, local(): lax.psum_scatter(own_qkv, 'rep', scatter_dimension=1, tiled=True)  70.7 us
    all_gather x1, waiting for transfers between devices, local(): lax.all_gather(up_weight, 'shard', axis=0, tiled=True)  60 us
    psum x1, blocking collectives, local(): lax.psum((own_qv, own_outb, own_g1, own_s1, own_upb, own_downb, own_g2, o...  58.5 us
    all_gather x1, waiting for transfers between devices, local(): lax.all_gather(banded[2], 'rep', axis=1, tiled=True)  49.4 us
  transfers between devices with their start and end apart: 20, of which 18 were waited for; matrix products, arithmetic and copies ran while one was open for 9% of the time, Pallas kernels for 0%

commit v1 on v0

--- a/solution.py
+++ b/solution.py
@@ -3,6 +3,8 @@
 import jax
 import jax.numpy as jnp
 from jax import lax
+from jax.experimental import pallas as pl
+from jax.experimental.pallas import tpu as pltpu
 from jax.sharding import PartitionSpec as P
 
 HEADS = 12
@@ -307,9 +309,579 @@
     )
 
 
+LOW = jnp.bfloat16
+FULL = jnp.float32
+MESH = pl.DeviceIdType.MESH
+BLOCK = 384
+CHUNKS = 12
+HOPS = 9
+VMEM_GRANT = 60 * 1024 * 1024
+
+
+def greet(partners):
+    barrier = pltpu.get_barrier_semaphore()
+    for partner in partners:
+        pl.semaphore_signal(barrier, inc=1, device_id=partner, device_id_type=MESH)
+    pl.semaphore_wait(barrier, len(partners))
+
+
+def places():
+    rep = lax.axis_index("rep")
+    y = lax.axis_index("shard")
+    core = lax.rem(rep, 2)
+    x = lax.rem(rep // 2, 2)
+    z0 = lax.rem(rep // 4, 2)
+    z1 = rep // 8
+    partners = {
+        "core": {"rep": rep + 1 - 2 * core},
+        "x": {"rep": rep + 2 - 4 * x},
+        "z0": {"rep": rep + 4 - 8 * z0},
+        "z1": {"rep": rep + 8 - 16 * z1},
+        "y": {"shard": 1 - y},
+    }
+    return core, x, y, z0, z1, partners
+
+
+def gather_kernel(
+    x_in, g_in, s_in, q_in, o_in, u_in, d_in,
+    x_out, g_out, s_out, q_out, o_out, u_out, d_out,
+    send, recv, near,
+):
+    core, x, y, _, _, partners = places()
+    rows = x_in.shape[1]
+    used = [0]
+
+    def remote(src, dst, way):
+        spot = used[0]
+        used[0] += 1
+        return pltpu.make_async_remote_copy(
+            src_ref=src,
+            dst_ref=dst,
+            send_sem=send.at[spot],
+            recv_sem=recv.at[spot],
+            device_id=partners[way],
+            device_id_type=MESH,
+        )
+
+    greet([partners["y"], partners["x"], partners["core"]])
+
+    pieces = []
+    for src, dst, parts in ((q_in, q_out, 1), (o_in, o_out, 1), (u_in, u_out, 2), (d_in, d_out, 2)):
+        height = src.shape[0]
+        size = height // 4 // parts
+        for part in range(parts):
+            pieces.append((src, dst, height, size, part * size))
+
+    def spot_of(height, size, shift, shard, x_of):
+        quarter = 2 * x_of + core
+        return pl.ds(shard * height + quarter * (height // 4) + shift, size)
+
+    singles = [
+        remote(s_in, s_out.at[y], "y"),
+        remote(x_in.at[1 - y], x_out.at[pl.ds(y * rows, rows)], "y"),
+    ]
+    for copy in singles:
+        copy.start()
+    over_y = []
+    for src, dst, height, size, shift in pieces:
+        copy = remote(
+            src.at[spot_of(height, size, shift, 0, x)],
+            dst.at[spot_of(height, size, shift, y, x)],
+            "y",
+        )
+        copy.start()
+        over_y.append(copy)
+    last = remote(g_in.at[1 - y], g_out.at[pl.ds(y * rows, rows)], "y")
+    last.start()
+    singles.append(last)
+
+    locals_ = [
+        (s_in, s_out.at[y]),
+        (x_in.at[y], x_out.at[pl.ds(y * rows, rows)]),
+        (q_in, q_out.at[pl.ds(y * q_in.shape[0], q_in.shape[0])]),
+        (o_in, o_out.at[pl.ds(y * o_in.shape[0], o_in.shape[0])]),
+        (u_in, u_out.at[pl.ds(y * u_in.shape[0], u_in.shape[0])]),
+        (d_in, d_out.at[pl.ds(y * d_in.shape[0], d_in.shape[0])]),
+        (g_in.at[y], g_out.at[pl.ds(y * rows, rows)]),
+    ]
+    locals_ = [pltpu.make_async_copy(a, b, near.at[i]) for i, (a, b) in enumerate(locals_)]
+    for copy in locals_:
+        copy.start()
+
+    over_x = []
+    over_core = []
+    for index in range(len(pieces) + 1):
+        if index < len(pieces):
+            _, dst, height, size, shift = pieces[index]
+            over_y[index].wait()
+            block = dst.at[spot_of(height, size, shift, 1 - y, x)]
+            copy = remote(block, block, "x")
+            copy.start()
+            over_x.append(copy)
+            copy = remote(block, block, "core")
+            copy.start()
+            over_core.append(copy)
+        if index > 0:
+            _, dst, height, size, shift = pieces[index - 1]
+            over_x[index - 1].wait()
+            block = dst.at[spot_of(height, size, shift, 1 - y, 1 - x)]
+            copy = remote(block, block, "core")
+            copy.start()
+            over_core.append(copy)
+    for copy in singles + over_core + locals_:
+        copy.wait()
+
+
+def gather_call(x, g, s, q, o, u, d):
+    def doubled(a):
+        return jax.ShapeDtypeStruct((2 * a.shape[0],) + a.shape[1:], a.dtype)
+
+    tokens = jax.ShapeDtypeStruct((x.shape[0] * x.shape[1], x.shape[2]), x.dtype)
+    smalls = jax.ShapeDtypeStruct((2,) + s.shape, s.dtype)
+    anywhere = pl.BlockSpec(memory_space=pl.ANY)
+    return pl.pallas_call(
+        gather_kernel,
+        out_shape=(tokens, tokens, smalls, doubled(q), doubled(o), doubled(u), doubled(d)),
+        in_specs=[anywhere] * 7,
+        out_specs=[anywhere] * 7,
+        scratch_shapes=[
+            pltpu.SemaphoreType.DMA((27,)),
+            pltpu.SemaphoreType.DMA((27,)),
+            pltpu.SemaphoreType.DMA((7,)),
+        ],
+        compiler_params=pltpu.CompilerParams(collective_id=0, has_side_effects=True),
+    )(x, g, s, q, o, u, d)
+
+
+def reduce_kernel(
+    low1, gh, act, gb, flat, gqkv, mixed, ga, smalls, ig,
+    up_out, down_out, qkv_out, out_out, smalls_out, ig_out,
+    parts, got_core, got_y, got_x, got_z0, got_z1, whole, small_now, small_sum, small_got,
+    send, recv, small_send, small_recv, ig_send, ig_recv, near,
+):
+    core, x, y, z0, z1, partners = places()
+    rows = ig.shape[0] // 2
+
+    greet([partners[way] for way in ("core", "x", "y", "z0", "z1")])
+
+    ig_copy = pltpu.make_async_remote_copy(
+        src_ref=ig.at[pl.ds((1 - y) * rows, rows)],
+        dst_ref=ig_out,
+        send_sem=ig_send,
+        recv_sem=ig_recv,
+        device_id=partners["y"],
+        device_id_type=MESH,
+    )
+    ig_copy.start()
+
+    row_x = x * 192
+    row_z0 = row_x + z0 * 96
+    row_z1 = row_z0 + z1 * 48
+
+    def hop(stage, k):
+        if stage == 0:
+            pair = (parts.at[k, 1 - core], got_core.at[k], "core")
+        elif stage == 1:
+            pair = (parts.at[k, core, 1 - y], got_y.at[k], "y")
+        elif stage == 2:
+            pair = (parts.at[k, core, y, pl.ds((1 - x) * 192, 192)], got_x.at[k], "x")
+        elif stage == 3:
+            pair = (parts.at[k, core, y, pl.ds(row_x + (1 - z0) * 96, 96)], got_z0.at[k], "z0")
+        elif stage == 4:
+            pair = (parts.at[k, core, y, pl.ds(row_z0 + (1 - z1) * 48, 48)], got_z1.at[k], "z1")
+        elif stage == 5:
+            block = whole.at[k, core, pl.ds(row_z1, 48)]
+            pair = (block, block, "z1")
+        elif stage == 6:
+            block = whole.at[k, core, pl.ds(row_z0, 96)]
+            pair = (block, block, "z0")
+        elif stage == 7:
+            block = whole.at[k, core, pl.ds(row_x, 192)]
+            pair = (block, block, "x")
+        else:
+            block = whole.at[k, core]
+            pair = (block, block, "core")
+        return pltpu.make_async_remote_copy(
+            src_ref=pair[0],
+            dst_ref=pair[1],
+            send_sem=send.at[stage, k],
+            recv_sem=recv.at[stage, k],
+            device_id=partners[pair[2]],
+            device_id_type=MESH,
+        )
+
+    def product(k, left, left_spots, right, right_spot):
+        for half in range(2):
+            lhs = left[:, pl.ds(left_spots[half], BLOCK)]
+            for side in range(2):
+                spot = right_spot + side * BLOCK
+                if not isinstance(spot, int):
+                    spot = pl.multiple_of(spot, 128)
+                rhs = right[:, pl.ds(spot, BLOCK)]
+                parts[k, side, half] = lax.dot_general(
+                    lhs, rhs, (((0,), (0,)), ((), ())), preferred_element_type=FULL
+                ).astype(LOW)
+
+    def store(k, wait):
+        def go(out, row, column):
+            for side in range(2):
+                copy = pltpu.make_async_copy(
+                    whole.at[k, side],
+                    out.at[pl.ds(row, BLOCK), pl.ds(pl.multiple_of(column + side * BLOCK, 128), BLOCK)],
+                    near.at[k, side],
+                )
+                if wait:
+                    copy.wait()
+                else:
+                    copy.start()
+
+        @pl.when(k < 4)
+        def _():
+            go(up_out, 0, k * 768)
+
+        @pl.when((k >= 4) & (k < 8))
+        def _():
+            go(down_out, (k - 4) * BLOCK, 0)
+
+        @pl.when((k >= 8) & (k < 11))
+        def _():
+            go(qkv_out, 0, (k - 8) * 768)
+
+        @pl.when(k == 11)
+        def _():
+            go(out_out, 0, 0)
+
+    def compute(k):
+        @pl.when(k < 4)
+        def _():
+            product(k, low1, (0, BLOCK), gh, k * 768)
+
+        @pl.when((k >= 4) & (k < 8))
+        def _():
+            spot = pl.multiple_of((k - 4) * BLOCK, 128)
+            product(k, act, (spot, pl.multiple_of(spot + 4 * BLOCK, 128)), gb, 0)
+
+        @pl.when((k >= 8) & (k < 11))
+        def _():
+            product(k, flat, (0, BLOCK), gqkv, (k - 8) * 768)
+
+        @pl.when(k == 11)
+        def _():
+            product(k, mixed, (0, BLOCK), ga, 0)
+
+    def act_on(stage, k):
+        if stage == 0:
+            compute(k)
+        else:
+            hop(stage - 1, k).wait()
+        if stage == 1:
+            for half in range(2):
+                parts[k, core, half] = parts[k, core, half] + got_core[k, half]
+        elif stage == 2:
+            parts[k, core, y] = parts[k, core, y] + got_y[k]
+        elif stage == 3:
+            spot = pl.ds(pl.multiple_of(row_x, 16), 192)
+            parts[k, core, y, spot] = parts[k, core, y, spot] + got_x[k]
+        elif stage == 4:
+            spot = pl.ds(pl.multiple_of(row_z0, 16), 96)
+            parts[k, core, y, spot] = parts[k, core, y, spot] + got_z0[k]
+        elif stage == 5:
+            spot = pl.ds(pl.multiple_of(row_z1, 16), 48)
+            whole[k, core, spot] = parts[k, core, y, spot] + got_z1[k]
+        if stage < HOPS:
+            hop(stage, k).start()
+        else:
+            store(k, False)
+
+    small_now[...] = smalls[...]
+    small_ways = ("core", "y", "x", "z0", "z1")
+
+    def small_hop(stage):
+        if stage == 0:
+            src, dst = small_now, small_got.at[0]
+        elif stage == 1:
+            src, dst = small_now.at[1 - y], small_got.at[1, 0]
+        else:
+            src, dst = small_sum.at[stage - 2], small_got.at[stage, 0]
+        return pltpu.make_async_remote_copy(
+            src_ref=src,
+            dst_ref=dst,
+            send_sem=small_send.at[stage],
+            recv_sem=small_recv.at[stage],
+            device_id=partners[small_ways[stage]],
+            device_id_type=MESH,
+        )
+
+    def small_step(stage):
+        if stage > 0:
+            small_hop(stage - 1).wait()
+        if stage == 1:
+            small_now[...] = small_now[...] + small_got[0]
+        elif stage == 2:
+            small_sum[0] = small_now[y] + small_got[1, 0]
+        elif stage in (3, 4):
+            small_sum[stage - 2] = small_sum[stage - 3] + small_got[stage - 1, 0]
+        elif stage == 5:
+            smalls_out[...] = small_sum[2] + small_got[4, 0]
+        if stage < 5:
+            small_hop(stage).start()
+
+    def turn(t, carry):
+        for stage in range(HOPS + 1):
+            @pl.when((t >= stage) & (t < stage + CHUNKS))
+            def _(stage=stage):
+                act_on(stage, t - stage)
+
+        for stage in range(6):
+            @pl.when(t == stage)
+            def _(stage=stage):
+                small_step(stage)
+
+        return carry
+
+    lax.fori_loop(0, CHUNKS + HOPS, turn, 0)
+
+    def finish(k, carry):
+        store(k, True)
+        return carry
+
+    lax.fori_loop(0, CHUNKS, finish, 0)
+    ig_copy.wait()
+
+
+def reduce_call(low1, gh, act, gb, flat, gqkv, mixed, ga, smalls, ig):
+    width = flat.shape[1]
+    inside = pl.BlockSpec(memory_space=pltpu.VMEM)
+    anywhere = pl.BlockSpec(memory_space=pl.ANY)
+    half = (ig.shape[0] // 2, width)
+    return pl.pallas_call(
+        reduce_kernel,
+        out_shape=(
+            jax.ShapeDtypeStruct((width // 2, gh.shape[1]), LOW),
+            jax.ShapeDtypeStruct((act.shape[1] // 2, width), LOW),
+            jax.ShapeDtypeStruct((width // 2, gqkv.shape[1]), LOW),
+            jax.ShapeDtypeStruct((width // 2, width), LOW),
+            jax.ShapeDtypeStruct(smalls.shape[1:], FULL),
+            jax.ShapeDtypeStruct(half, LOW),
+        ),
+        in_specs=[inside] * 10,
+        out_specs=[anywhere] * 4 + [inside, anywhere],
+        scratch_shapes=[
+            pltpu.VMEM((CHUNKS, 2, 2, BLOCK, BLOCK), LOW),
+            pltpu.VMEM((CHUNKS, 2, BLOCK, BLOCK), LOW),
+            pltpu.VMEM((CHUNKS, BLOCK, BLOCK), LOW),
+            pltpu.VMEM((CHUNKS, 192, BLOCK), LOW),
+            pltpu.VMEM((CHUNKS, 96, BLOCK), LOW),
+            pltpu.VMEM((CHUNKS, 48, BLOCK), LOW),
+            pltpu.VMEM((CHUNKS, 2, BLOCK, BLOCK), LOW),
+            pltpu.VMEM(smalls.shape, FULL),
+            pltpu.VMEM((3,) + smalls.shape[1:], FULL),
+            pltpu.VMEM((5,) + smalls.shape, FULL),
+            pltpu.SemaphoreType.DMA((HOPS, CHUNKS)),
+            pltpu.SemaphoreType.DMA((HOPS, CHUNKS)),
+            pltpu.SemaphoreType.DMA((5,)),
+            pltpu.SemaphoreType.DMA((5,)),
+            pltpu.SemaphoreType.DMA,
+            pltpu.SemaphoreType.DMA,
+            pltpu.SemaphoreType.DMA((CHUNKS, 2)),
+        ],
+        compiler_params=pltpu.CompilerParams(
+            collective_id=1, has_side_effects=True, vmem_limit_bytes=VMEM_GRANT
+        ),
+    )(low1, gh, act, gb, flat, gqkv, mixed, ga, smalls, ig)
+
+
+def whole_sequence(
+    inputs,
+    doc_lengths,
+    qkv_weight,
+    qv_bias,
+    out_weight,
+    out_bias,
+    first_gain,
+    first_shift,
+    up_weight,
+    up_bias,
+    down_weight,
+    down_bias,
+    second_gain,
+    second_shift,
+    grad_out,
+):
+    seqs, rows, width = inputs.shape
+    full_len = seqs * rows
+    y = lax.axis_index("shard")
+    head_dim = width // HEADS
+    scale = 1.0 / math.sqrt(head_dim)
+    vectors = (
+        qv_bias, out_bias, first_gain, first_shift, up_bias, down_bias, second_gain, second_shift
+    )
+    sizes = [v.shape[0] for v in vectors]
+    packed = jnp.concatenate(vectors).reshape(12, BLOCK)
+    packed = jnp.pad(packed, ((0, 4), (0, 0)))
+    flat, cotangent, smalls, full_qkv, full_out, full_up, full_down = gather_call(
+        inputs, grad_out, packed, qkv_weight, out_weight, up_weight, down_weight
+    )
+    smalls = smalls[:, :12].reshape(2, 12 * BLOCK).astype(FULL)
+    whole = []
+    start = 0
+    for size in sizes:
+        whole.append(smalls[:, start : start + size].reshape(2 * size))
+        start += size
+    full_qv, full_outb, full_g1, full_s1, full_upb, full_downb, full_g2, full_s2 = whole
+    lengths = lax.dynamic_index_in_dim(doc_lengths, y, 0, keepdims=False)
+    ends = jnp.cumsum(lengths)
+    spots = jnp.arange(full_len, dtype=jnp.int32)
+    docs = jnp.sum((ends[:, None] <= spots[None, :]).astype(jnp.int32), axis=0)
+    bias = jnp.concatenate([full_qv[:width], jnp.zeros((width,), FULL), full_qv[width:]])
+    qkv = (jnp.dot(flat, full_qkv, preferred_element_type=FULL) + bias).astype(LOW)
+
+    def heads_of(values):
+        return values.reshape(full_len, HEADS, head_dim).transpose(1, 0, 2)
+
+    query = heads_of(qkv[:, :width])
+    keys = heads_of(qkv[:, width : 2 * width])
+    values = heads_of(qkv[:, 2 * width :])
+    mixed, logsum = attend_forward(query, keys, values, docs, scale)
+    mixed_flat = mixed.transpose(1, 0, 2).reshape(full_len, width)
+    attended = jnp.dot(mixed_flat, full_out, preferred_element_type=FULL) + full_outb
+    first_norm, first_normed, first_scaler = norm_forward(
+        flat.astype(FULL) + attended, full_g1, full_s1
+    )
+    first_low = first_norm.astype(LOW)
+    hidden = jnp.dot(first_low, full_up, preferred_element_type=FULL) + full_upb
+    normal_cdf = 0.5 * (1.0 + lax.erf(hidden * 0.7071067811865476))
+    active = (hidden * normal_cdf).astype(LOW)
+    branch = jnp.dot(active, full_down, preferred_element_type=FULL) + full_downb
+    second_out, second_normed, second_scaler = norm_forward(first_norm + branch, full_g2, full_s2)
+    layer_own = second_out.astype(LOW).reshape(seqs, rows, width)
+    swap = [(0, 1), (1, 0)]
+    layer_got = lax.ppermute(
+        lax.dynamic_index_in_dim(layer_own, 1 - y, 0, keepdims=False), "shard", swap
+    )
+    cotangent = cotangent.astype(FULL)
+    second_gain_grad = jnp.sum(cotangent * second_normed, axis=0)
+    second_shift_grad = jnp.sum(cotangent, axis=0)
+    grad_second = norm_backward(cotangent, second_normed, second_scaler, full_g2)
+    grad_branch = grad_second.astype(LOW)
+    down_bias_grad = column_sums(grad_branch)
+    grad_active = jnp.einsum("td,fd->tf", grad_branch, full_down, preferred_element_type=FULL)
+    normal_pdf = jnp.exp(-0.5 * hidden * hidden) * 0.3989422804014327
+    grad_hidden = (grad_active * (normal_cdf + hidden * normal_pdf)).astype(LOW)
+    up_bias_grad = column_sums(grad_hidden)
+    grad_first_norm = grad_second + jnp.einsum(
+        "tf,df->td", grad_hidden, full_up, preferred_element_type=FULL
+    )
+    first_gain_grad = jnp.sum(grad_first_norm * first_normed, axis=0)
+    first_shift_grad = jnp.sum(grad_first_norm, axis=0)
+    grad_first = norm_backward(grad_first_norm, first_normed, first_scaler, full_g1)
+    grad_attended = grad_first.astype(LOW)
+    out_bias_grad = column_sums(grad_attended)
+    grad_mixed = jnp.einsum(
+        "te,de->td", grad_attended, full_out, preferred_element_type=FULL
+    ).astype(LOW)
+    grad_query, grad_keys, grad_values = attend_backward(
+        query, keys, values, docs, logsum, heads_of(grad_mixed), scale
+    )
+
+    def flat_of(values):
+        return values.transpose(1, 0, 2).reshape(full_len, width)
+
+    grad_qkv = jnp.concatenate(
+        [flat_of(grad_query), flat_of(grad_keys), flat_of(grad_values)], axis=1
+    )
+    qkv_sums = column_sums(grad_qkv)
+    qv_bias_grad = jnp.concatenate([qkv_sums[:width], qkv_sums[2 * width :]])
+    input_grad = grad_first + jnp.einsum(
+        "te,de->td", grad_qkv, full_qkv, preferred_element_type=FULL
+    )
+    small_grads = (
+        qv_bias_grad,
+        out_bias_grad,
+        first_gain_grad,
+        first_shift_grad,
+        up_bias_grad,
+        down_bias_grad,
+        second_gain_grad,
+        second_shift_grad,
+    )
+    small_grads = jnp.concatenate([v.reshape(2, -1) for v in small_grads], axis=1)
+    small_grads = jnp.pad(small_grads.reshape(2, 6, width), ((0, 0), (0, 2), (0, 0)))
+    up_sum, down_sum, qkv_sum, out_sum, small_sum, grad_got = reduce_call(
+        first_low,
+        grad_hidden,
+        active,
+        grad_branch,
+        flat,
+        grad_qkv,
+        mixed_flat,
+        grad_attended,
+        small_grads,
+        input_grad.astype(LOW),
+    )
+    small_sum = small_sum[:6].reshape(6 * width)
+    sums = []
+    start = 0
+    for size in sizes:
+        sums.append(small_sum[start : start + size])
+        start += size
+
+    def both(own, got):
+        own = lax.dynamic_index_in_dim(own, y, 0, keepdims=False)
+        first = jnp.where(y == 0, own, got)
+        second = jnp.where(y == 0, got, own)
+        return jnp.stack([first, second])
+
+    layer_out = both(layer_own, layer_got)
+    input_grad = both(input_grad.reshape(seqs, rows, width), grad_got.astype(FULL))
+    return (
+        layer_out,
+        input_grad,
+        qkv_sum.astype(FULL),
+        sums[0],
+        out_sum.astype(FULL),
+        sums[1],
+        sums[2],
+        sums[3],
+        up_sum.astype(FULL),
+        sums[4],
+        down_sum.astype(FULL),
+        sums[5],
+        sums[6],
+        sums[7],
+    )
+
+
+def attend_forward(query, keys, values, docs, scale):
+    scores = jnp.einsum("hqd,hkd->hqk", query, keys, preferred_element_type=FULL) * scale
+    same = (docs[:, None] == docs[None, :])[None]
+    masked = jnp.where(same, scores, -1000000000.0)
+    top = jnp.max(masked, axis=-1, keepdims=True)
+    expo = jnp.exp(masked - top)
+    total = jnp.sum(expo, axis=-1, keepdims=True)
+    probs_low = (expo / total).astype(LOW)
+    mixed = jnp.einsum("hqk,hkd->hqd", probs_low, values, preferred_element_type=FULL)
+    return mixed.astype(LOW), top + jnp.log(total)
+
+
+def attend_backward(query, keys, values, docs, logsum, grad, scale):
+    scores = jnp.einsum("hqd,hkd->hqk", query, keys, preferred_element_type=FULL) * scale
+    same = (docs[:, None] == docs[None, :])[None]
+    probs = jnp.where(same, jnp.exp(scores - logsum), 0.0)
+    grad_probs = jnp.einsum("hqd,hkd->hqk", grad, values, preferred_element_type=FULL)
+    probs_low = probs.astype(LOW)
+    inner = jnp.sum(probs * grad_probs, axis=-1, keepdims=True)
+    grad_scores = (probs * (grad_probs - inner)).astype(LOW)
+    grad_query = jnp.einsum("hqk,hkd->hqd", grad_scores, keys, preferred_element_type=FULL) * scale
+    grad_keys = jnp.einsum("hqk,hqd->hkd", grad_scores, query, preferred_element_type=FULL) * scale
+    grad_values = jnp.einsum("hqk,hqd->hkd", probs_low, grad, preferred_element_type=FULL)
+    return grad_query.astype(LOW), grad_keys.astype(LOW), grad_values.astype(LOW)
+
+
 def solution(mesh):
+    shape = (mesh.shape["rep"], mesh.shape["shard"])
     return jax.shard_map(
-        local,
+        whole_sequence if shape == (16, 2) else local,
         mesh=mesh,
         in_specs=(
             P("rep", "shard", None),

time: 1270 us -> 498 us (0.39)
  waiting for transfers between devices: 962 us -> 0.01 us
  Pallas kernels: 0 us -> 367 us
  blocking collectives: 103 us -> 0 us
  local copies, waits for them, and re-layouts: 65.3 us -> 24 us
  matrix products: 98.3 us -> 59.7 us
  other arithmetic: 19.3 us -> 35.1 us
  between operations: 17.3 us -> 1.78 us
    reduce_scatter x7 -> x0, waiting for transfers between devices: 462 us -> none  [the longest x1 113 us: local(): lax.psum_scatter(up_weight_grad, 'shard', scatter_dimension=0, tiled=True)]
    pallas_call x0 -> x2, Pallas kernels: none -> 367 us  [the longest x1 243 us: gather_call(): pl.pallas_call(gather_kernel, out_shape=(tokens, tokens, smalls, doubled(...]
    all_gather x10 -> x0, waiting for transfers between devices: 281 us -> none  [the longest x1 60 us: local(): lax.all_gather(up_weight, 'shard', axis=0, tiled=True)]
    unnamed x23 -> x0, waiting for transfers between devices: 218 us -> none
    psum x1 -> x0, blocking collectives: 58.5 us -> none  [local(): lax.psum((own_qv, own_outb, own_g1, own_s1, own_upb, own_downb, own_g2, o...]
    dot_general x26 -> x14, matrix products: 98.3 us -> 59.7 us  [the longest x1 9.5 us: attend_backward(): jnp.einsum('hqd,hkd->hqk', grad, values, preferred_element_type=FULL)]
    all_gather x8 -> x0, blocking collectives: 35.7 us -> none  [the longest x1 5.24 us: local(): lax.all_gather(qv_bias, 'shard', axis=0, tiled=True)]
    unnamed x85, local copies, waits for them, and re-layouts: 43.6 us -> 10.1 us
  transfers between devices with their start and end apart: 20 -> 1, of which waited for: 18 -> 0; matrix products, arithmetic and copies ran while one was open for 9% -> 15% of each run, Pallas kernels for 0% -> 25%
where the time goes in v1:
time: 498 us; the launch traced here: 489 us
  Pallas kernels  367 us (74%)
  matrix products  59.7 us (12%)
  other arithmetic  35.1 us (7%)
  local copies, waits for them, and re-layouts  24 us (5%)
    pallas_call x1, Pallas kernels, gather_call(): pl.pallas_call(gather_kernel, out_shape=(tokens, tokens, smalls, doubled(...  243 us
    pallas_call x1, Pallas kernels, reduce_call(): pl.pallas_call(reduce_kernel, out_shape=(jax.ShapeDtypeStruct((width // 2...  124 us
    unnamed x85, local copies, waits for them, and re-layouts  10.1 us
  transfers between devices with their start and end apart: 1, of which 0 were waited for; matrix products, arithmetic and copies ran while one was open for 15% of the time, Pallas kernels for 25%

profile of v1, /device:TPU:0, one launch (start us, length us, event | category | flops | bytes accessed | tf_op | source)
XLA Modules:
  0.0 489.3 jit_solution(9331318865941962994)
XLA Ops:
  0.7 0.9 dynamic-update-slice.8
  1.5 0.9 dynamic-update-slice.9
  2.4 0.9 dynamic-update-slice.10
  3.3 0.9 dynamic-update-slice.11
  4.1 0.9 dynamic-update-slice.12
  5.0 0.9 dynamic-update-slice.13
  5.8 0.9 dynamic-update-slice.14
  6.7 0.9 dynamic-update-slice.15
  8.2 243.2 %shard_map.254 = (bf16[512,768]{1,0:T(8,128)(2,1)}, bf16[512,768]{1,0:T(8,128)(2,1)}, bf16[2,16,384]{2,1,0:T(8,128)(2,1)}, bf16[768,2304]{1,0:T(8,128)(2,1)}, bf...) custom-call(bf16[2,256,768]{2,1,0:T(8,128)(2,1)} %x_in.1, bf16[2,256,768]{2,1,0:T(8,128)(2,1)} %g_in.1, ...), custom_call_target="tpu_custom_call" | custom-call | tf_op jit(solution)/shard_map/pallas_call | solution.py:442
  252.9 4.2 fusion.12
  258.2 2.1 select_reduce_fusion
  260.4 2.6 fusion
  263.0 2.0 copy-done.2
  264.9 3.7 fusion.23
  268.7 0.9 fusion.40
  270.4 0.8 slice-done.3
  271.4 4.9 multiply_convert_fusion.1
  276.2 2.8 fusion.41
  279.4 1.9 fusion.19
  281.3 2.9 convert_reduce_fusion.3
  284.2 0.9 copy-done.13
  285.1 0.8 dynamic-slice_bitcast_fusion
  285.9 1.5 collective-permute-start
  287.4 2.3 copy.64.mixed
  289.7 7.6 %convert_reduce_fusion = (f32[3072]{0:T(1024)S(1)}, bf16[512,3072]{1,0:T(8,128)(2,1)S(1)}) fusion(f32[512,3072]{1,0:T(8,128)} %get-tuple-element.84, f32[3072]{0:T(1024)S(1)} %add.130, bf16[512,768]{1,0:T(8,128)(2,1)} %get-tuple-element.51.gb, bf16[3072,768]{1,0:T(8,128)(2,1)} %get-tuple-element.32), kind=kOutput, calls=%fused_computation.15 | convolution fusion | flops 2436363264 | bytes 14966784 | tf_op jit(solution)/shard_map/td,fd->tf/dot_general | solution.py:768
  297.4 6.9 %multiply_reduce_fusion.1 = (f32[768]{0:T(1024)S(1)}, f32[512]{0:T(512)S(1)}, f32[512]{0:T(512)S(1)}, f32[768]{0:T(1024)S(1)}, f32[512,768]{1,0:T(8,128)S(1)}) fusion(f32[512,768]{1,0:T(8,128)S(1)} %get-tuple-element.82, f32[512]{0:T(512)S(1)} %add_rsqrt_fusion.1, f32[512]{0:T(512)S(1)} %broadcast_multiply_fusion.5, f32[768]{0:T(1024)S(1)} %mul.154, ...), kind=kOutput, calls=%fused_computation.37 | convolution fusion | flops 2422994432 | bytes 13398016 | tf_op jit(solution)/shard_map/tf,df->td/dot_general | solution.py:772
  304.3 1.7 convert_reduce_fusion.4
  306.0 0.8 convolution_convert_fusion
  307.1 6.2 %fusion.20 = bf16[12,512,64]{1,2,0:T(8,128)(2,1)S(1)} fusion(bf16[12,512,64]{1,2,0:T(8,128)(2,1)S(1)} %bitcast.88, f32[12,512,512]{1,2,0:T(8,128)} %copy-done.2, f32[12,512]{1,0:T(8,128)S(1)} %log_add_fusion, pred[512,512]{0,1:T(8,128)(4,1)S(1)} %broadcast_compare_fusion), kind=kOutput, calls=%fused_computation.54 | convolution fusion | flops 415629312 | bytes 14442496 | tf_op jit(solution)/shard_map/hqk,hqd->hkd/dot_general | solution.py:877
  313.4 9.5 %multiply_reduce_fusion = (f32[12,512]{1,0:T(8,128)S(1)}, f32[12,512,512]{1,2,0:T(8,128)}) fusion(f32[12,512,512]{1,2,0:T(8,128)} %copy-done.2, f32[12,512]{1,0:T(8,128)S(1)} %log_add_fusion, pred[512,512]{0,1:T(8,128)(4,1)S(1)} %broadcast_compare_fusion, bf16[12,512,64]{1,2,0:T(8,128)(2,1)S(1)} %bitcast.89, bf16[12,512,64]{1,2,0:T(8,128)(2,1)S(1)} %bitcast.87), kind=kOutput, calls=%fused_computation.1 | convolution fusion | flops 418375680 | bytes 27049984 | tf_op jit(solution)/shard_map/hqd,hkd->hqk/dot_general | solution.py:871
  322.9 7.6 %multiply_convert_fusion = bf16[12,512,512]{1,2,0:T(8,128)(2,1)S(1)} fusion(f32[12,512,512]{1,2,0:T(8,128)} %get-tuple-element.89, f32[12,512,512]{1,2,0:T(8,128)S(1)} %bitcast.80, f32[12,512]{1,0:T(8,128)S(1)} %get-tuple-element.88, f32[12,512]{1,0:T(8,128)S(1)} %log_add_fusion, pred[512,512]{0,1:T(8,128)(4,1)S(1)} %broadcast_compare_fusion), kind=kLoop, calls=%fused_computation | loop fusion | flops 18874368 | bytes 31768576 | tf_op jit(solution)/shard_map/convert_element_type | solution.py:874
  330.5 2.9 multiply_convert_fusion.2
  333.4 1.1 multiply_convert_fusion.3
  334.9 1.2 copy.61
  336.1 2.3 copy.62
  338.4 1.8 convert_reduce_fusion.1
  340.4 0.8 pad.9.smalls
  341.2 5.9 %fusion.42 = (bf16[512,768]{1,0:T(8,128)(2,1)}, f32[512,768]{1,0:T(8,128)}) fusion(f32[512,768]{1,0:T(8,128)} %get-tuple-element.54, bf16[512,2304]{1,0:T(8,128)(2,1)S(1)} %get-tuple-element.56.gqkv, bf16[768,2304]{1,0:T(8,128)(2,1)} %get-tuple-element.28), kind=kOutput, calls=%fused_computation.107 | convolution fusion | flops 1812725760 | bytes 9830400 | tf_op jit(solution)/shard_map/te,de->td/dot_general | solution.py:795
  347.1 124.0 %shard_map.255 = (bf16[384,3072]{1,0:T(8,128)(2,1)}, bf16[1536,768]{1,0:T(8,128)(2,1)}, bf16[384,2304]{1,0:T(8,128)(2,1)}, bf16[384,768]{1,0:T(8,128)(2,1)}, f32[8,768]{1,0:T(8,128)}, /*index=5*/bf16[256,768]{1,0:T(8,128)(2,1)}) custom-call(bf16[512,768]{1,0:T(8,128)(2,1)} %copy-done.10, bf16[512,3072]{1,0:T(8,128)(2,1)} %copy-done.12, ...), custom_call_target="tpu_custom_call" | custom-call | tf_op jit(solution)/shard_map/pallas_call | solution.py:657
  471.1 1.5 fusion.25
  472.6 1.3 slice_reduce_fusion.2
  475.3 2.3 convert_element_type.141
  477.6 2.0 convert_element_type.140
  479.7 2.8 convert_element_type.142
  482.4 2.5 convert_element_type.143
  485.0 1.2 pad_maximum_fusion.1
  486.8 1.1 fusion.27
  487.9 0.9 pad_maximum_fusion.2
  (131 shorter events, 7.0 us)
Async XLA Ops:
  0.6 251.6 %copy-start = (s32[2,4]{1,0:T(2,128)S(1)}, s32[2,4]{1,0:T(2,128)}, u32[]{:S(2)}) copy-start(s32[2,4]{1,0:T(2,128)} %param.16) | copy-start | bytes 100
  257.6 2.7 copy-start.3
  257.9 5.0 %copy-start.8 = (bf16[512,768]{0,1:T(8,128)(2,1)}, bf16[512,768]{0,1:T(8,128)(2,1)S(1)}, u32[]{:S(2)}) copy-start(bf16[512,768]{0,1:T(8,128)(2,1)S(1)} %copy.55) | copy-start | bytes 2359300
  258.2 2.1 copy-start.6
  260.4 4.6 copy-start.2
  264.9 3.8 copy-start.20
  264.9 3.8 copy-start.26
  268.7 1.3 copy-start.21
  268.7 2.5 slice-start.3
  268.7 2.6 slice-start.4
  270.0 6.2 %slice-start.5 = ((s8[4718592]{0:T(1024)(128)(4,1)}), s8[4194304]{0:T(1024)(128)(4,1)S(1)}, s32[]{:S(2)}) async-start(s8[4718592]{0:T(1024)(128)(4,1)} %bitcast.104), calls=%async_computation.5 | async-start | bytes 8388608
  270.3 5.9 %copy-start.10 = (bf16[512,768]{1,0:T(8,128)(2,1)}, bf16[512,768]{1,0:T(8,128)(2,1)S(1)}, u32[]{:S(2)}) copy-start(bf16[512,768]{1,0:T(8,128)(2,1)S(1)} %fusion.24.low1) | copy-start | bytes 2359300
  271.4 4.9 slice-start.6
  276.2 2.8 copy-start.11
  281.3 6.1 %copy-start.22 = (f32[512]{0:T(512)}, f32[512]{0:T(512)S(1)}, u32[]{:S(2)}) copy-start(f32[512]{0:T(512)S(1)} %get-tuple-element.94) | copy-start | bytes 6148
  281.3 6.1 %copy-start.24 = (f32[512]{0:T(512)}, f32[512]{0:T(512)S(1)}, u32[]{:S(2)}) copy-start(f32[512]{0:T(512)S(1)} %get-tuple-element.95) | copy-start | bytes 6148
  284.2 0.9 copy-start.13
  285.9 200.9 %collective-permute-start = (bf16[256,768]{1,0:T(8,128)(2,1)}, bf16[256,768]{1,0:T(8,128)(2,1)}, u32[]{:S(2)}, u32[]{:S(2)}) collective-permute-start(bf16[256,768]{1,0:T(8,128)(2,1)} %dynamic-slice_bitcast_fusion), channel_id=1, source_target_pairs={{0,1},{1,0},{2,3},{3,2},{4,5},{5,4},{6,7},{7,6},{8,9},{9,8},{10,11... | collective-permute-start | bytes 1179656 | tf_op jit(solution)/shard_map/ppermute | solution.py:759
  289.7 7.6 %copy-start.15 = (bf16[512,768]{1,0:T(8,128)(2,1)S(1)}, bf16[512,768]{1,0:T(8,128)(2,1)}, u32[]{:S(2)}) copy-start(bf16[512,768]{1,0:T(8,128)(2,1)} %get-tuple-element.33) | copy-start | bytes 2359300
  289.7 7.6 %copy-start.23 = (f32[512]{0:T(512)S(1)}, f32[512]{0:T(512)}, u32[]{:S(2)}) copy-start(f32[512]{0:T(512)} %copy-done.22) | copy-start | bytes 6148
  289.7 7.6 %copy-start.25 = (f32[512]{0:T(512)S(1)}, f32[512]{0:T(512)}, u32[]{:S(2)}) copy-start(f32[512]{0:T(512)} %copy-done.24) | copy-start | bytes 6148
  297.3 6.9 %copy-start.12 = (bf16[512,3072]{1,0:T(8,128)(2,1)}, bf16[512,3072]{1,0:T(8,128)(2,1)S(1)}, u32[]{:S(2)}) copy-start(bf16[512,3072]{1,0:T(8,128)(2,1)S(1)} %get-tuple-element.91.gh) | copy-start | bytes 9437188
  304.3 1.7 copy-start.27
  306.0 7.4 %copy-start.16 = (bf16[512,768]{1,0:T(8,128)(2,1)}, bf16[512,768]{1,0:T(8,128)(2,1)S(1)}, u32[]{:S(2)}) copy-start(bf16[512,768]{1,0:T(8,128)(2,1)S(1)} %get-tuple-element.53.ga) | copy-start | bytes 2359300
  307.1 6.3 %copy-start.9 = (bf16[512,768]{0,1:T(8,128)(2,1)S(1)}, bf16[512,768]{0,1:T(8,128)(2,1)}, u32[]{:S(2)}) copy-start(bf16[512,768]{0,1:T(8,128)(2,1)} %copy-done.8) | copy-start | bytes 2359300
  307.1 15.8 %slice-start = ((s8[12582912]{0:T(1024)(128)(4,1)}), s8[4194304]{0:T(1024)(128)(4,1)S(1)}, s32[]{:S(2)}) async-start(s8[12582912]{0:T(1024)(128)(4,1)} %bitcast.79), calls=%async_computation | async-start | bytes 8388608
  307.1 15.8 %slice-start.1 = ((s8[12582912]{0:T(1024)(128)(4,1)}), s8[4194304]{0:T(1024)(128)(4,1)S(1)}, s32[]{:S(2)}) async-start(s8[12582912]{0:T(1024)(128)(4,1)} %bitcast.79), calls=%async_computation.1 | async-start | bytes 8388608
  313.4 9.5 %slice-start.2 = ((s8[12582912]{0:T(1024)(128)(4,1)}), s8[4194304]{0:T(1024)(128)(4,1)S(1)}, s32[]{:S(2)}) async-start(s8[12582912]{0:T(1024)(128)(4,1)} %bitcast.79), calls=%async_computation.2 | async-start | bytes 8388608
  322.9 7.6 %copy-start.7 = (bf16[512,768]{0,1:T(8,128)(2,1)S(1)}, bf16[512,768]{0,1:T(8,128)(2,1)}, u32[]{:S(2)}) copy-start(bf16[512,768]{0,1:T(8,128)(2,1)} %copy-done.6) | copy-start | bytes 2359300
  330.5 2.9 copy-start.4
  340.2 6.9 %copy-start.5 = (bf16[512,2304]{1,0:T(8,128)(2,1)}, bf16[512,2304]{1,0:T(8,128)(2,1)S(1)}, u32[]{:S(2)}) copy-start(bf16[512,2304]{1,0:T(8,128)(2,1)S(1)} %get-tuple-element.56.gqkv) | copy-start | bytes 7077892
  471.1 6.5 %copy-start.19 = (bf16[384,2304]{1,0:T(8,128)(2,1)S(1)}, bf16[384,2304]{1,0:T(8,128)(2,1)}, u32[]{:S(2)}) copy-start(bf16[384,2304]{1,0:T(8,128)(2,1)} %get-tuple-element.35) | copy-start | bytes 5308420
  475.3 4.3 copy-start.18
  479.7 2.8 copy-start.17
  485.0 1.9 copy-start.14
  485.0 3.9 copy-start.1
